TPU v7x, 32 devices: a whole 2x2x4 slice. The times are simulated.
32 devices in a mesh: pairs: 8 (over y, x, core), day: 4 (over z).
Axes of the slice: x: 2, y: 2, z: 4, core: 2. Of those that a mesh axis runs over, the one named last changes fastest.
Arguments:
- spectra: bfloat16 [4, 2, 256, 18432], P('day', None, 'pairs'), may hold values from -6 to 6
- station_row: int32 [256], replicated, may hold values from 0 to 255, as said below
- needed: int32 [128], P('pairs'), may hold values from 0 to 255, as said below
- pair_list: int32 [512, 2], P('pairs'), may hold values from 0 to 15, as said below
- counts: int32 [8], P('pairs'), may hold values from 32 to 64, as said below
Outputs:
- correlations: float32 [512, 1024], P(('pairs', 'day'))
Inputs may be any that keep to these rules, and one draw needn't show every extreme that they name: `station_row`: A permutation of the stations: each row of the spectra belongs to exactly one station. `needed`: each block's 16 entries are distinct stations; at most 4 of one block's stations have their rows on any one index of pairs, and in every block some index of pairs holds exactly 4 of them. `pair_list`: the two positions of a slot differ; empty slots also hold valid positions. `counts`: the live slots of a block are its first ones; in every draw some block has all 64 slots live.
All inputs are finite; a program needn't handle non-finite values.
Results may differ from a plain program's by a relative error of at most 0.013.
Values may be sent and summed in bfloat16 or wider, within the bound.
A program may use at most 128 MiB of HBM per device.

v0:
```python
import math
import jax
import jax.numpy as jnp
from jax import lax
from jax.sharding import PartitionSpec as P

F = 18432
LAGS = 1024
KLO = 720
NFFT = 72000
CAP = 4
TWO_PI = 2.0 * math.pi
FLOOR = 0.25


def angle_rows(first_bin, width):
    bins_here = first_bin + jnp.arange(width, dtype=jnp.int32)
    shifts = jnp.arange(LAGS, dtype=jnp.int32) - LAGS // 2
    phases = jnp.mod(bins_here[:, None] * shifts[None, :], NFFT).astype(jnp.float32) * (
        TWO_PI / NFFT
    )
    return (jnp.cos(phases), jnp.sin(phases))


def to_lags(stack_real, stack_imag, bin_start):
    width_all = stack_real.shape[1]
    block_width = math.gcd(width_all, 512)
    low_cos, low_sin = angle_rows(0, block_width)

    def add_block(index, total):
        offset = index * block_width
        high_cos, high_sin = angle_rows(KLO + bin_start + offset, 1)
        cosine = (high_cos * low_cos - high_sin * low_sin).astype(jnp.bfloat16)
        sine = (high_sin * low_cos + high_cos * low_sin).astype(jnp.bfloat16)
        part_real = lax.dynamic_slice_in_dim(stack_real, offset, block_width, 1)
        part_imag = lax.dynamic_slice_in_dim(stack_imag, offset, block_width, 1)
        total = total + jnp.dot(part_real, cosine, preferred_element_type=jnp.float32)
        return total - jnp.dot(part_imag, sine, preferred_element_type=jnp.float32)

    empty = jnp.zeros((stack_real.shape[0], LAGS), jnp.float32)
    total = lax.fori_loop(0, width_all // block_width, add_block, empty)
    return total * (8.0 / math.sqrt(F))


def owner_ranks(owners):
    length = owners.shape[-1]
    earlier = jnp.arange(length)[None, :] < jnp.arange(length)[:, None]
    same = owners[..., :, None] == owners[..., None, :]
    return jnp.sum(jnp.logical_and(same, earlier), axis=-1)


def make_stack(sums, first_slot, live_count, days):
    slots_here = first_slot + jnp.arange(sums.shape[0], dtype=jnp.int32)
    live = (slots_here < live_count).astype(jnp.float32)[:, None]
    coherence = (sums[:, 2] * sums[:, 2] + sums[:, 3] * sums[:, 3]) / (days * days)
    factor = coherence * live
    stack_real = (sums[:, 0] / days * factor).astype(jnp.bfloat16)
    stack_imag = (sums[:, 1] / days * factor).astype(jnp.bfloat16)
    return (stack_real, stack_imag)


def day_terms(left, right):
    cross_real = left[0] * right[0] + left[1] * right[1]
    cross_imag = left[1] * right[0] - left[0] * right[1]
    divisor = jnp.maximum(jnp.sqrt(cross_real * cross_real + cross_imag * cross_imag), FLOOR)
    return jnp.stack([cross_real, cross_imag, cross_real / divisor, cross_imag / divisor], axis=1)


def shards(spectra, station_row, needed, pair_list, counts):
    holders = lax.axis_size("pairs")
    days_here = lax.axis_size("day")
    stations_here = spectra.shape[2]
    slot_count = pair_list.shape[0]
    my_rows = station_row[needed]
    my_owner = my_rows // stations_here
    my_rank = owner_ranks(my_owner)
    my_slot = my_owner * CAP + my_rank
    onehot = my_slot[:, None] == jnp.arange(holders * CAP, dtype=jnp.int32)[None, :]
    asked = jnp.sum(jnp.where(onehot, (my_rows % stations_here)[:, None], 0), axis=0)
    wanted = lax.all_to_all(
        asked.reshape(holders, CAP), "pairs", split_axis=0, concat_axis=0, tiled=True
    )
    day_count = spectra.shape[0]
    bins_all = spectra.shape[3]
    outgoing = jnp.take(spectra, wanted.reshape(-1), axis=2).reshape(
        day_count, 2, holders, CAP, bins_all
    )
    incoming = lax.all_to_all(outgoing, "pairs", split_axis=2, concat_axis=2, tiled=True)
    mine_spec = jnp.take(incoming.reshape(day_count, 2, holders * CAP, bins_all), my_slot, axis=2)
    first = jnp.take(mine_spec, pair_list[:, 0], axis=2)
    second = jnp.take(mine_spec, pair_list[:, 1], axis=2)
    share = slot_count // days_here
    live_count = counts[0]
    left = first[0].astype(jnp.float32)
    right = second[0].astype(jnp.float32)
    sums = lax.psum_scatter(
        day_terms(left, right).astype(jnp.bfloat16), "day", scatter_dimension=0, tiled=True
    ).astype(jnp.float32)
    first_slot = lax.axis_index("day") * share
    stack_real, stack_imag = make_stack(sums, first_slot, live_count, days_here)
    return to_lags(stack_real, stack_imag, 0)


def solution(mesh):
    in_specs = (P("day", None, "pairs", None), P(), P("pairs"), P("pairs", None), P("pairs"))
    out_specs = P(("pairs", "day"), None)
    return jax.shard_map(shards, mesh=mesh, in_specs=in_specs, out_specs=out_specs, check_vma=False)
```

profile of v0, /device:TPU:0, one launch (start us, length us, event | category | flops | bytes accessed | tf_op | source)
XLA Modules:
  0.0 1182.2 jit_solution(6503301249137884689)
XLA Ops:
  37.3 28.6 %all-to-all-done.1 = bf16[1,2,8,4,18432]{4,1,3,0,2:T(2,128)(2,1)S(1)} async-done(((bf16[1,2,8,4,18432]{4,1,3,0,2:T(2,128)(2,1)}), bf16[1,2,8,4,18432]{4,1,3,0,2:T(2,128)(2,1)S(1)}, u32[]{:S(2)}, u32[]{:S(2)}) %all-to-all-start.1) | async-done | bytes 2359328 | tf_op jit(solution)/shard_map/all_to_all | solution.py:88
  70.0 11.8 gather_fusion.3
  81.7 11.8 gather_fusion.4
  93.6 16.3 %fusion.40 = (f32[1,2,64,18432]{3,2,1,0:T(8,128)}, f32[1,2,64,18432]{3,2,1,0:T(8,128)}) fusion(bf16[64,2,18432]{2,1,0:T(2,128)(2,1)} %gather_fusion.4, pred[64]{0:T(512)(128)(4,1)S(1)} %copy-done.3, bf16[64,2,18432]{2,1,0:T(2,128)(2,1)} %gather_fusion.3, pred[64]{0:T(512)(128)(4,1)S(1)} %copy-done.2), kind=kLoop, calls=%fused_computation.49 | loop fusion | flops 9437184 | bytes 28311680 | tf_op jit(solution)/shard_map/convert_element_type | solution.py:95
  130.4 322.2 %all-reduce.3.cloned.1.call-done = bf16[64,4,18432]{2,1,0:T(4,128)(2,1)} async-done(((bf16[64,4,18432]{2,1,0:T(4,128)(2,1)}), bf16[64,4,18432]{2,1,0:T(4,128)(2,1)}) %all-reduce.3.cloned.1.call-update) | async-done | bytes 9437200
  459.7 714.9 %while.19 = (s32[]{:T(128)}, f32[16,1024]{1,0:T(8,128)S(1)}, bf16[16,18432]{1,0:T(8,128)(2,1)S(1)}, bf16[16,18432]{1,0:T(8,128)(2,1)S(1)}, s32[1024]{0:T(1024)S(...) while((s32[]{:T(128)}, f32[16,1024]{1,0:T(8,128)S(1)}, ...), condition=%wide.region_4.6_spmd.clone.clone.clone.clone, body=%wide.region_3.5_spmd.clone.clone.clone.clone.sunk | while | flops 47245320 | bytes 327861 | solution.py:41
  459.8 9.9 convolution_add_fusion.2
  469.7 9.9 convolution_subtract_fusion.2
  479.7 9.9 convolution_add_fusion.2
  489.6 9.9 convolution_subtract_fusion.2
  499.5 9.9 convolution_add_fusion.2
  509.4 9.9 convolution_subtract_fusion.2
  519.4 9.9 convolution_add_fusion.2
  539.2 9.9 convolution_add_fusion.2
  549.2 9.9 convolution_subtract_fusion.2
  559.1 9.9 convolution_add_fusion.2
  569.0 9.9 convolution_subtract_fusion.2
  579.0 9.9 convolution_add_fusion.2
  588.9 9.9 convolution_subtract_fusion.2
  598.8 9.9 convolution_add_fusion.2
  608.7 9.9 convolution_subtract_fusion.2
  618.7 9.9 convolution_add_fusion.2
  628.6 9.9 convolution_subtract_fusion.2
  638.5 9.9 convolution_add_fusion.2
  648.4 9.9 convolution_subtract_fusion.2
  658.4 9.9 convolution_add_fusion.2
  668.3 9.9 convolution_subtract_fusion.2
  678.3 9.9 convolution_add_fusion.2
  688.2 9.9 convolution_subtract_fusion.2
  698.1 9.9 convolution_add_fusion.2
  708.0 9.9 convolution_subtract_fusion.2
  718.0 9.9 convolution_add_fusion.2
  727.9 9.9 convolution_subtract_fusion.2
  737.8 9.9 convolution_add_fusion.2
  747.7 9.9 convolution_subtract_fusion.2
  757.7 9.9 convolution_add_fusion.2
  767.6 9.9 convolution_subtract_fusion.2
  777.5 9.9 convolution_add_fusion.2
  787.4 9.9 convolution_subtract_fusion.2
  797.4 9.9 convolution_add_fusion.2
  807.3 9.9 convolution_subtract_fusion.2
  817.3 9.9 convolution_add_fusion.2
  837.1 9.9 convolution_add_fusion.2
  847.0 9.9 convolution_subtract_fusion.2
  857.0 9.9 convolution_add_fusion.2
  866.9 9.9 convolution_subtract_fusion.2
  876.8 9.9 convolution_add_fusion.2
  886.7 9.9 convolution_subtract_fusion.2
  896.7 9.9 convolution_add_fusion.2
  916.5 9.9 convolution_add_fusion.2
  926.5 9.9 convolution_subtract_fusion.2
  936.4 9.9 convolution_add_fusion.2
  946.3 9.9 convolution_subtract_fusion.2
  956.3 9.9 convolution_add_fusion.2
  976.1 9.9 convolution_add_fusion.2
  996.0 9.9 convolution_add_fusion.2
  1015.8 9.9 convolution_add_fusion.2
  1035.7 9.9 convolution_add_fusion.2
  1055.6 9.9 convolution_add_fusion.2
  1075.4 9.9 convolution_add_fusion.2
  1095.3 9.9 convolution_add_fusion.2
  1115.1 9.9 convolution_add_fusion.2
  1135.0 9.9 convolution_add_fusion.2
  1154.8 9.9 convolution_add_fusion.2
  (105 shorter events, 202.1 us)
Async XLA Ops:
  6.5 0.7 copy-start
  8.9 10.7 all-to-all-start
  32.2 4.6 copy-start.4
  32.2 33.8 %all-to-all-start.1 = ((bf16[1,2,8,4,18432]{4,1,3,0,2:T(2,128)(2,1)}), bf16[1,2,8,4,18432]{4,1,3,0,2:T(2,128)(2,1)S(1)}, u32[]{:S(2)}, u32[]{:S(2)}) async-start(bf16[1,2,8,4,18432]{4,1,3,0,2:T(2,128)(2,1)} %broadcast_select_fusion), calls=%async_computation.1 | async-start | bytes 4718592 | tf_op jit(solution)/shard_map/all_to_all | solution.py:88
  36.5 416.1 %all-reduce.3.cloned.1.call-start = ((), (), s32[]{:S(2)}) async-start(), calls=%async_computation.2 | async-start | bytes 18874368
  81.7 11.8 copy-start.2
  81.7 11.8 copy-start.3
  128.3 0.7 copy-start.5
  1174.6 0.7 copy-start.1
Sparse Core Ops, SparseCore 0:
  128.5 324.0 all-reduce.2
where the time goes:
time: 1180 us
  matrix products  712 us (60%)
  waiting for transfers between devices  351 us (30%)
  local copies, waits for them, and re-layouts  49.7 us (4%)
  other arithmetic  44.2 us (4%)
  between operations  14.9 us (1%)
    dot_general x36, matrix products, add_block(): jnp.dot(part_real, cosine, preferred_element_type=jnp.float32)  357 us
    dot_general x36, matrix products, add_block(): return total - jnp.dot(part_imag, sine, preferred_element_type=jnp.float32)  356 us
    unnamed x2, waiting for transfers between devices  322 us
    all_to_all x1, waiting for transfers between devices, shards(): lax.all_to_all(outgoing, 'pairs', split_axis=2, concat_axis=2, tiled=True)  28.6 us
  transfers between devices with their start and end apart: 3, of which 2 were waited for; matrix products, arithmetic and copies ran while one was open for 1% of the time, Pallas kernels for 0%

commit v1 on v0

--- a/solution.py
+++ b/solution.py
@@ -85,7 +85,13 @@
     outgoing = jnp.take(spectra, wanted.reshape(-1), axis=2).reshape(
         day_count, 2, holders, CAP, bins_all
     )
-    incoming = lax.all_to_all(outgoing, "pairs", split_axis=2, concat_axis=2, tiled=True)
+    clear_vector = lambda local_block: jnp.concatenate(
+        lax.all_to_all(
+            jnp.stack(jnp.split(local_block, lax.axis_size("pairs"), axis=2), axis=0), "pairs", 0, 0
+        ),
+        axis=2,
+    )
+    incoming = clear_vector(outgoing)
     mine_spec = jnp.take(incoming.reshape(day_count, 2, holders * CAP, bins_all), my_slot, axis=2)
     first = jnp.take(mine_spec, pair_list[:, 0], axis=2)
     second = jnp.take(mine_spec, pair_list[:, 1], axis=2)

time: 1180 us -> 1180 us (level)
    convert_element_type x1, other arithmetic: 16.3 us -> 3.04 us  [shards(): right = second[0].astype(jnp.float32)]
where the time goes in v1:
time: 1180 us
  matrix products  712 us (60%)
  waiting for transfers between devices  351 us (30%)
  local copies, waits for them, and re-layouts  57.2 us (5%)
  other arithmetic  34.5 us (3%)
  between operations  14.9 us (1%)
    dot_general x36, matrix products, add_block(): jnp.dot(part_real, cosine, preferred_element_type=jnp.float32)  357 us
    dot_general x36, matrix products, add_block(): return total - jnp.dot(part_imag, sine, preferred_element_type=jnp.float32)  356 us
    unnamed x2, waiting for transfers between devices  322 us
    all_to_all x1, waiting for transfers between devices, shards(): lax.all_to_all(jnp.stack(jnp.split(local_block, lax.axis_size('pairs'), a...  28.6 us
  transfers between devices with their start and end apart: 3, of which 2 were waited for; matrix products, arithmetic and copies ran while one was open for 1% of the time, Pallas kernels for 0%

profile of v1, /device:TPU:0, one launch (start us, length us, event | category | flops | bytes accessed | tf_op | source)
XLA Modules:
  0.0 1180.0 jit_solution(1083958754235201050)
XLA Ops:
  43.3 28.6 %all-to-all-done.1 = bf16[8,1,2,1,4,18432]{5,2,4,3,1,0:T(2,128)(2,1)S(1)} async-done(((bf16[8,1,2,1,4,18432]{5,2,4,3,1,0:T(2,128)(2,1)}), bf16[8,1,2,1,4,18432]{5,2,4,3,1,0:T(2,128)(2,1)S(1)}, u32[]{:S(2)}, u32[]{:S(2)}) %all-to-all-start.1) | async-done | bytes 2359328 | tf_op jit(solution)/shard_map/all_to_all | solution.py:89
  75.9 11.9 %gather_fusion.3 = bf16[64,2,18432]{2,1,0:T(2,128)(2,1)} fusion(bf16[2,16,18432]{2,0,1:T(2,128)(2,1)S(1)} %fusion.54, s32[1024]{0:T(1024)S(1)} %get-tuple-element.283), kind=kCustom, calls=%fused_computation.clone | custom fusion | bytes 9437440 | tf_op jit(solution)/shard_map/jit(_take)/gather | solution.py:96
  87.8 11.8 %gather_fusion.4 = bf16[64,2,18432]{2,1,0:T(2,128)(2,1)} fusion(bf16[2,16,18432]{2,0,1:T(2,128)(2,1)S(1)} %fusion.54, s32[1024]{0:T(1024)S(1)} %get-tuple-element.282), kind=kCustom, calls=%fused_computation.1.clone | custom fusion | bytes 9437440 | tf_op jit(solution)/shard_map/jit(_take)/gather | solution.py:97
  128.1 322.3 %all-reduce.3.cloned.1.call-done = bf16[64,4,18432]{2,1,0:T(4,128)(2,1)} async-done(((bf16[64,4,18432]{2,1,0:T(4,128)(2,1)}), bf16[64,4,18432]{2,1,0:T(4,128)(2,1)}) %all-reduce.3.cloned.1.call-update) | async-done | bytes 9437200
  457.6 714.9 %while.19 = (s32[]{:T(128)}, f32[16,1024]{1,0:T(8,128)S(1)}, bf16[16,18432]{1,0:T(8,128)(2,1)S(1)}, bf16[16,18432]{1,0:T(8,128)(2,1)S(1)}, s32[1024]{0:T(1024)S(...) while((s32[]{:T(128)}, f32[16,1024]{1,0:T(8,128)S(1)}, ...), condition=%wide.region_4.6_spmd.clone.clone.clone.clone, body=%wide.region_3.5_spmd.clone.clone.clone.clone.sunk | while | flops 47245320 | bytes 327861 | solution.py:41
  457.7 9.9 convolution_add_fusion.2
  467.6 9.9 convolution_subtract_fusion.2
  477.5 9.9 convolution_add_fusion.2
  497.4 9.9 convolution_add_fusion.2
  507.3 9.9 convolution_subtract_fusion.2
  517.2 9.9 convolution_add_fusion.2
  527.1 9.9 convolution_subtract_fusion.2
  537.1 9.9 convolution_add_fusion.2
  547.0 9.9 convolution_subtract_fusion.2
  557.0 9.9 convolution_add_fusion.2
  566.9 9.9 convolution_subtract_fusion.2
  576.8 9.9 convolution_add_fusion.2
  586.7 9.9 convolution_subtract_fusion.2
  596.7 9.9 convolution_add_fusion.2
  606.6 9.9 convolution_subtract_fusion.2
  616.5 9.9 convolution_add_fusion.2
  626.4 9.9 convolution_subtract_fusion.2
  636.4 9.9 convolution_add_fusion.2
  646.3 9.9 convolution_subtract_fusion.2
  656.3 9.9 convolution_add_fusion.2
  666.2 9.9 convolution_subtract_fusion.2
  676.1 9.9 convolution_add_fusion.2
  686.0 9.9 convolution_subtract_fusion.2
  696.0 9.9 convolution_add_fusion.2
  705.9 9.9 convolution_subtract_fusion.2
  715.8 9.9 convolution_add_fusion.2
  725.7 9.9 convolution_subtract_fusion.2
  735.7 9.9 convolution_add_fusion.2
  745.6 9.9 convolution_subtract_fusion.2
  755.5 9.9 convolution_add_fusion.2
  765.4 9.9 convolution_subtract_fusion.2
  775.4 9.9 convolution_add_fusion.2
  795.3 9.9 convolution_add_fusion.2
  805.2 9.9 convolution_subtract_fusion.2
  815.1 9.9 convolution_add_fusion.2
  825.0 9.9 convolution_subtract_fusion.2
  835.0 9.9 convolution_add_fusion.2
  844.9 9.9 convolution_subtract_fusion.2
  854.8 9.9 convolution_add_fusion.2
  874.7 9.9 convolution_add_fusion.2
  884.6 9.9 convolution_subtract_fusion.2
  894.5 9.9 convolution_add_fusion.2
  904.5 9.9 convolution_subtract_fusion.2
  914.4 9.9 convolution_add_fusion.2
  924.3 9.9 convolution_subtract_fusion.2
  934.3 9.9 convolution_add_fusion.2
  944.2 9.9 convolution_subtract_fusion.2
  954.1 9.9 convolution_add_fusion.2
  964.0 9.9 convolution_subtract_fusion.2
  974.0 9.9 convolution_add_fusion.2
  993.8 9.9 convolution_add_fusion.2
  1013.7 9.9 convolution_add_fusion.2
  1033.6 9.9 convolution_add_fusion.2
  1053.4 9.9 convolution_add_fusion.2
  1073.3 9.9 convolution_add_fusion.2
  1093.1 9.9 convolution_add_fusion.2
  1113.0 9.9 convolution_add_fusion.2
  1132.8 9.9 convolution_add_fusion.2
  1152.7 9.9 convolution_add_fusion.2
  (119 shorter events, 206.2 us)
Async XLA Ops:
  6.5 0.7 copy-start
  8.9 10.7 all-to-all-start
  38.1 4.6 copy-start.7
  38.1 33.8 %all-to-all-start.1 = ((bf16[8,1,2,1,4,18432]{5,2,4,3,1,0:T(2,128)(2,1)}), bf16[8,1,2,1,4,18432]{5,2,4,3,1,0:T(2,128)(2,1)S(1)}, u32[]{:S(2)}, u32[]{:S(2)}) async-start(bf16[8,1,2,1,4,18432]{5,2,4,3,1,0:T(2,128)(2,1)} %fusion.55), calls=%async_computation.1 | async-start | bytes 4718592 | tf_op jit(solution)/shard_map/all_to_all | solution.py:89
  42.4 408.0 %all-reduce.3.cloned.1.call-start = ((), (), s32[]{:S(2)}) async-start(), calls=%async_computation.2 | async-start | bytes 18874368
  87.8 11.8 %copy-start.6 = (pred[64]{0:T(512)(128)(4,1)S(1)}, pred[64]{0:T(512)(128)(4,1)}, u32[]{:S(2)}) copy-start(pred[64]{0:T(512)(128)(4,1)} %get-tuple-element.260) | copy-start | bytes 196
  99.6 5.5 copy-start.2
  99.6 5.5 copy-start.5
  113.0 4.2 copy-start.3
  113.0 4.2 copy-start.4
  126.2 0.7 copy-start.8
  1172.5 0.7 copy-start.1
Sparse Core Ops, SparseCore 0:
  126.3 324.0 all-reduce.2
